TPU v7x, 32 devices: a whole 2x2x4 slice. The times are simulated.
32 devices in a mesh: dp: 8 (over z, core), expert: 4 (over y, x).
Axes of the slice: x: 2, y: 2, z: 4, core: 2. Of those that a mesh axis runs over, the one named last changes fastest.
Arguments:
- tokens: bfloat16 [4, 1024, 3584], P('expert', 'dp'), may hold values from -6 to 6
- grad_out: bfloat16 [4, 1024, 3584], P('expert', 'dp'), may hold values from -6 to 6
- route_ids: int32 [4, 1024], P('expert', 'dp'), may hold values from 0 to 3, as said below
- route_gates: float32 [4, 1024], P('expert', 'dp'), may hold values from 0.2 to 1
- w_gate: bfloat16 [4, 3584, 1024], P('expert', 'dp'), may hold values from -0.09375 to 0.09375
- w_up: bfloat16 [4, 3584, 1024], P('expert', 'dp'), may hold values from -0.09375 to 0.09375
- w_down: bfloat16 [4, 1024, 3584], P('expert', 'dp'), may hold values from -0.1875 to 0.1875
Outputs:
- moe_out: bfloat16 [4, 1024, 3584], P('expert', 'dp')
- input_grad: bfloat16 [4, 1024, 3584], P('expert', None, 'dp')
- gate_grad: float32 [4, 1024], P('expert', 'dp')
Inputs may be any that keep to these rules, and one draw needn't show every extreme that they name: `route_ids`: among the 128 tokens of one device at most 80 name the same expert; one expert is named by exactly 80 tokens of every device; on one device the counts of the other experts differ by at most one.
All inputs are finite; a program needn't handle non-finite values.
Results may differ from a plain program's by a relative error of at most 0.0057.
Values may be sent and summed in bfloat16 or wider, within the bound.
A program may use at most 128 MiB of HBM per device.

v0:
```python
import jax
import jax.numpy as jnp
from jax import lax
from jax.sharding import PartitionSpec as P

F32 = jnp.float32
BF16 = jnp.bfloat16
DOWN_PARTS = 2


def placement(route_line, expert_count, capacity):
    tok_count = route_line.shape[0]
    same = route_line[:, None] == route_line[None, :]
    earlier = jnp.arange(tok_count)[None, :] < jnp.arange(tok_count)[:, None]
    placed = jnp.sum((same & earlier).astype(jnp.int32), axis=1)
    slots = route_line * capacity + placed
    rows = jnp.arange(expert_count * capacity, dtype=jnp.int32)
    return (rows[:, None] == slots[None, :]).astype(BF16)


def mm(a, b, dims=(((1,), (0,)), ((), ()))):
    return lax.dot_general(a, b, dims, preferred_element_type=F32)


NT = (((1,), (1,)), ((), ()))
TN = (((0,), (0,)), ((), ()))


def local(tokens, grad_out, route_ids, route_gates, w_gate, w_up, w_down):
    expert_count = lax.axis_size("expert")
    dp_count = lax.axis_size("dp")
    tok_count = tokens.shape[1]
    width = tokens.shape[2]
    capacity = max(2, 5 * tok_count // (2 * expert_count))
    place = placement(route_ids[0], expert_count, capacity)
    own_grad = grad_out[0].astype(F32)
    gate_column = route_gates[0][:, None]
    scaled_grad = (gate_column * own_grad).astype(BF16)

    def over_experts(rows):
        cols = rows.shape[1]
        got = lax.all_to_all(
            rows.reshape(expert_count, capacity, cols),
            "expert",
            split_axis=0,
            concat_axis=0,
            tiled=True,
        )
        return got.reshape(expert_count * capacity, cols)

    gate_matrix = lax.all_gather(w_gate, "dp", axis=1, tiled=True)[0]
    up_matrix = lax.all_gather(w_up, "dp", axis=1, tiled=True)[0]
    w_down, _ = lax.optimization_barrier((w_down, gate_matrix[:16, :128]))
    step = width // DOWN_PARTS
    spans = [slice(i * step, (i + 1) * step) for i in range(DOWN_PARTS)]
    downs = [lax.all_gather(w_down[:, :, s], "dp", axis=1, tiled=True)[0] for s in spans]
    routed = over_experts(mm(place, tokens[0]).astype(BF16))
    routed_grad = over_experts(mm(place, scaled_grad).astype(BF16))
    gate_pre = mm(routed, gate_matrix)
    up_pre = mm(routed, up_matrix)
    sigmoid_gate = jax.nn.sigmoid(gate_pre)
    silu_gate = gate_pre * sigmoid_gate
    hidden = (silu_gate * up_pre).astype(BF16)
    moe_parts = []
    gate_grad = jnp.zeros((tok_count,), F32)
    hidden_grad = jnp.zeros_like(gate_pre)
    for s, down in zip(spans, downs):
        expert_out = mm(hidden, down).astype(BF16)
        hidden_grad = hidden_grad + mm(routed_grad[:, s], down, NT)
        token_out = mm(place, over_experts(expert_out), TN)
        moe_parts.append((gate_column * token_out).astype(BF16))
        gate_grad = gate_grad + jnp.sum(own_grad[:, s] * token_out, axis=1)
    moe_out = jnp.concatenate(moe_parts, axis=1)
    gate_pre_grad = (
        hidden_grad * up_pre * sigmoid_gate * (1.0 + gate_pre * (1.0 - sigmoid_gate))
    ).astype(BF16)
    up_pre_grad = (hidden_grad * silu_gate).astype(BF16)
    input_rows = (mm(gate_pre_grad, gate_matrix, NT) + mm(up_pre_grad, up_matrix, NT)).astype(BF16)
    home_rows = over_experts(input_rows)
    token_grad = mm(home_rows, place, TN).astype(BF16)
    parts = token_grad.reshape(dp_count, width // dp_count, tok_count)
    heads = lax.all_to_all(parts, "dp", split_axis=0, concat_axis=0, tiled=True)
    input_grad = heads.transpose(0, 2, 1).reshape(1, dp_count * tok_count, width // dp_count)
    return (moe_out[None], input_grad, gate_grad[None])


def solution(mesh):
    in_specs = (
        P("expert", "dp", None),
        P("expert", "dp", None),
        P("expert", "dp"),
        P("expert", "dp"),
        P("expert", "dp", None),
        P("expert", "dp", None),
        P("expert", "dp", None),
    )
    out_specs = (P("expert", "dp", None), P("expert", None, "dp"), P("expert", "dp"))
    return jax.shard_map(local, mesh=mesh, in_specs=in_specs, out_specs=out_specs, check_vma=False)
```

profile of v0, /device:TPU:0, one launch (start us, length us, event | category | flops | bytes accessed | tf_op | source)
XLA Modules:
  0.0 360.8 jit_solution(10377897107065206636)
XLA Ops:
  7.2 0.0 copy-start
  7.2 0.0 all-gather.11.cloned.1.call-start
  7.2 2.2 fusion.51
  9.4 0.0 all-gather.11.cloned.1.call-update
  9.5 0.0 all-gather.9.cloned.1.call-start
  9.5 0.7 all-gather.9.cloned.1.call-update
  10.2 0.0 all-gather.5.cloned.1.call-start
  10.3 0.7 all-gather.5.cloned.1.call-update
  10.9 0.0 all-gather.7.cloned.1.call-start
  11.0 0.5 all-gather.7.cloned.1.call-update
  11.5 0.2 convert_reduce_fusion
  11.7 2.3 convolution_convert_fusion
  14.0 5.2 %all-to-all-start.3 = ((bf16[4,80,3584]{2,1,0:T(8,128)(2,1)}), bf16[4,80,3584]{2,1,0:T(8,128)(2,1)S(1)}, u32[]{:S(2)}, u32[]{:S(2)}) async-start(bf16[4,80,3584]{2,1,0:T(8,128)(2,1)} %bitcast.17), calls=%async_computation.3 | async-start | bytes 4587520 | tf_op jit(solution)/shard_map/all_to_all | solution.py:42
  19.2 2.1 convolution_convert_fusion.1
  21.3 24.9 %all-to-all-done.3 = bf16[4,80,3584]{2,1,0:T(8,128)(2,1)S(1)} async-done(((bf16[4,80,3584]{2,1,0:T(8,128)(2,1)}), bf16[4,80,3584]{2,1,0:T(8,128)(2,1)S(1)}, u32[]{:S(2)}, u32[]{:S(2)}) %all-to-all-start.3) | async-done | bytes 2293792 | tf_op jit(solution)/shard_map/all_to_all | solution.py:42
  46.2 1.4 copy-done.5
  47.6 3.6 %all-to-all-start = ((bf16[4,80,3584]{2,1,0:T(8,128)(2,1)}), bf16[4,80,3584]{2,1,0:T(8,128)(2,1)S(1)}, u32[]{:S(2)}, u32[]{:S(2)}) async-start(bf16[4,80,3584]{2,1,0:T(8,128)(2,1)} %bitcast.5), calls=%async_computation | async-start | bytes 4587520 | tf_op jit(solution)/shard_map/all_to_all | solution.py:42
  51.3 4.3 %all-gather.11.cloned.1.call-done = bf16[1,1024,1792]{2,1,0:T(8,128)(2,1)} async-done(((bf16[1,128,1792]{2,1,0:T(8,128)(2,1)}), bf16[1,1024,1792]{2,1,0:T(8,128)(2,1)}) %all-gather.11.cloned.1.call-update) | async-done | bytes 3670032 | tf_op jit(solution)/shard_map/all_gather | solution.py:56
  55.6 4.8 %fusion.14 = f32[320,1024]{1,0:T(8,128)} fusion(bf16[1,1024,1792]{2,1,0:T(8,128)(2,1)} %all-gather.11.cloned.1.call-done, bf16[320,3584]{1,0:T(8,128)(2,1)} %bitcast.80), kind=kOutput, calls=%fused_computation.13 | convolution fusion | flops 1174405120 | bytes 6127616 | tf_op jit(solution)/shard_map/dot_general | solution.py:22
  60.4 38.9 %all-gather.9.cloned.1.call-done = bf16[1,1024,1792]{2,1,0:T(8,128)(2,1)} async-done(((bf16[1,128,1792]{2,1,0:T(8,128)(2,1)}), bf16[1,1024,1792]{2,1,0:T(8,128)(2,1)}) %all-gather.9.cloned.1.call-update) | async-done | bytes 3670032 | tf_op jit(solution)/shard_map/all_gather | solution.py:56
  99.3 5.2 %fusion.28 = f32[320,1024]{1,0:T(8,128)} fusion(f32[320,1024]{1,0:T(8,128)} %fusion.14, bf16[1,1024,1792]{2,1,0:T(8,128)(2,1)} %all-gather.9.cloned.1.call-done, bf16[320,3584]{1,0:T(8,128)(2,1)} %bitcast.81), kind=kOutput, calls=%fused_computation.24 | convolution fusion | flops 1174732800 | bytes 7438336 | tf_op jit(solution)/shard_map/dot_general | solution.py:22
  104.5 0.0 all-to-all-done
  104.5 68.7 %all-gather.5.cloned.1.call-done = bf16[1,3584,1024]{2,1,0:T(8,128)(2,1)} async-done(((bf16[1,448,1024]{2,1,0:T(8,128)(2,1)}), bf16[1,3584,1024]{2,1,0:T(8,128)(2,1)}) %all-gather.5.cloned.1.call-update) | async-done | bytes 7340048 | tf_op jit(solution)/shard_map/all_gather | solution.py:51
  173.2 6.7 %fusion.6 = f32[320,1024]{1,0:T(8,128)} fusion(bf16[320,3584]{1,0:T(8,128)(2,1)S(1)} %bitcast.78, bf16[1,3584,1024]{2,1,0:T(8,128)(2,1)} %all-gather.5.cloned.1.call-done), kind=kOutput, calls=%fused_computation.6 | convolution fusion | flops 2348810240 | bytes 10944512 | tf_op jit(solution)/shard_map/dot_general | solution.py:22
  179.9 66.9 %all-gather.7.cloned.1.call-done = bf16[1,3584,1024]{2,1,0:T(8,128)(2,1)} async-done(((bf16[1,448,1024]{2,1,0:T(8,128)(2,1)}), bf16[1,3584,1024]{2,1,0:T(8,128)(2,1)}) %all-gather.7.cloned.1.call-update) | async-done | bytes 7340048 | tf_op jit(solution)/shard_map/all_gather | solution.py:52
  246.8 7.2 %multiply_convert_fusion.3 = (bf16[320,1024]{1,0:T(8,128)(2,1)S(1)}, f32[320,1024]{1,0:T(8,128)}) fusion(f32[320,1024]{1,0:T(8,128)} %fusion.6, bf16[320,3584]{1,0:T(8,128)(2,1)S(1)} %bitcast.79, bf16[1,3584,1024]{2,1,0:T(8,128)(2,1)} %all-gather.7.cloned.1.call-done), kind=kOutput, calls=%fused_computation.27 | convolution fusion | flops 2350776320 | bytes 12910592 | tf_op jit(solution)/shard_map/dot_general | solution.py:22
  254.1 2.5 fusion.22
  256.5 3.7 %all-to-all-start.1 = ((bf16[4,80,1792]{2,1,0:T(8,128)(2,1)}), bf16[4,80,1792]{2,1,0:T(8,128)(2,1)S(1)}, u32[]{:S(2)}, u32[]{:S(2)}) async-start(bf16[4,80,1792]{2,1,0:T(8,128)(2,1)} %bitcast.10), calls=%async_computation.1 | async-start | bytes 2293760 | tf_op jit(solution)/shard_map/all_to_all | solution.py:42
  260.3 6.6 %fusion = f32[320,3584]{1,0:T(8,128)S(1)} fusion(bf16[1,3584,1024]{2,1,0:T(8,128)(2,1)} %all-gather.7.cloned.1.call-done, f32[320,1024]{1,0:T(8,128)} %fusion.28, f32[320,1024]{1,0:T(8,128)} %fusion.6), kind=kOutput, calls=%fused_computation | convolution fusion | flops 2350776320 | bytes 14548992 | tf_op jit(solution)/shard_map/dot_general | solution.py:22
  266.9 7.4 %fusion.11 = bf16[320,3584]{1,0:T(8,128)(2,1)} fusion(f32[320,3584]{1,0:T(8,128)S(1)} %fusion, bf16[1,3584,1024]{2,1,0:T(8,128)(2,1)} %all-gather.5.cloned.1.call-done, f32[320,1024]{1,0:T(8,128)S(1)} %copy-done.11, f32[320,1024]{1,0:T(8,128)S(1)} %copy-done.10, f32[320,1024]{1,0:T(8,128)S(1)} %copy-done.12), kind=kOutput, calls=%fused_computation.9 | convolution fusion | flops 2354380800 | bytes 18153472 | tf_op jit(solution)/shard_map/dot_general | solution.py:22
  274.3 1.1 all-to-all-done.1
  275.4 1.0 copy-done.1
  276.4 3.6 %all-to-all-start.4 = ((bf16[4,80,3584]{2,1,0:T(8,128)(2,1)}), bf16[4,80,3584]{2,1,0:T(8,128)(2,1)S(1)}, u32[]{:S(2)}, u32[]{:S(2)}) async-start(bf16[4,80,3584]{2,1,0:T(8,128)(2,1)} %bitcast.82), calls=%async_computation.4 | async-start | bytes 4587520 | tf_op jit(solution)/shard_map/all_to_all | solution.py:42
  280.0 4.6 %fusion.25 = bf16[320,1792]{1,0:T(8,128)(2,1)} fusion(bf16[320,1024]{1,0:T(8,128)(2,1)} %copy-done.9, bf16[1,1024,1792]{2,1,0:T(8,128)(2,1)} %all-gather.11.cloned.1.call-done), kind=kOutput, calls=%fused_computation.22 | convolution fusion | flops 1174978560 | bytes 5472256 | tf_op jit(solution)/shard_map/dot_general | solution.py:22
  284.6 22.0 %all-to-all-done.4 = bf16[4,80,3584]{2,1,0:T(8,128)(2,1)S(1)} async-done(((bf16[4,80,3584]{2,1,0:T(8,128)(2,1)}), bf16[4,80,3584]{2,1,0:T(8,128)(2,1)S(1)}, u32[]{:S(2)}, u32[]{:S(2)}) %all-to-all-start.4) | async-done | bytes 2293792 | tf_op jit(solution)/shard_map/all_to_all | solution.py:42
  306.6 4.3 %all-to-all-start.2 = ((bf16[4,80,1792]{2,1,0:T(8,128)(2,1)}), bf16[4,80,1792]{2,1,0:T(8,128)(2,1)}, u32[]{:S(2)}, u32[]{:S(2)}) async-start(bf16[4,80,1792]{2,1,0:T(8,128)(2,1)} %bitcast.83), calls=%async_computation.2 | async-start | bytes 2293760 | tf_op jit(solution)/shard_map/all_to_all | solution.py:42
  310.9 1.9 convolution_convert_fusion.2
  312.8 12.3 %all-to-all-done.2 = bf16[4,80,1792]{2,1,0:T(8,128)(2,1)} async-done(((bf16[4,80,1792]{2,1,0:T(8,128)(2,1)}), bf16[4,80,1792]{2,1,0:T(8,128)(2,1)}, u32[]{:S(2)}, u32[]{:S(2)}) %all-to-all-start.2) | async-done | bytes 1146912 | tf_op jit(solution)/shard_map/all_to_all | solution.py:42
  325.1 3.6 all-to-all-start.5
  328.7 0.2 bitcast_convert_fusion
  328.8 1.1 copy-done.2
  329.9 0.4 fusion.41
  330.4 1.9 fusion.34
  332.3 0.5 add_bitcast_fusion
  332.8 1.0 maximum_bitcast_fusion
  333.8 18.6 %all-to-all-done.5 = bf16[8,448,128]{2,1,0:T(8,128)(2,1)S(1)} async-done(((bf16[8,448,128]{2,1,0:T(8,128)(2,1)}), bf16[8,448,128]{2,1,0:T(8,128)(2,1)S(1)}, u32[]{:S(2)}, u32[]{:S(2)}) %all-to-all-start.5) | async-done | bytes 917536 | tf_op jit(solution)/shard_map/all_to_all | solution.py:82
  352.3 0.6 copy.11
  352.9 1.3 reshape.70
  (23 shorter events, 0.0 us)
Async XLA Ops:
  7.2 12.0 %copy-start = (bf16[1,128,3584]{2,1,0:T(8,128)(2,1)S(1)}, bf16[1,128,3584]{2,1,0:T(8,128)(2,1)}, u32[]{:S(2)}) copy-start(bf16[1,128,3584]{2,1,0:T(8,128)(2,1)} %param.7) | copy-start | bytes 2752516
  7.2 48.4 %all-gather.11.cloned.1.call-start = ((), (), s32[]{:S(2)}) async-start(), calls=%async_computation.9 | async-start | bytes 4128768 | tf_op jit(solution)/shard_map/all_gather | solution.py:56
  9.4 2.1 copy-start.8
  9.4 2.3 copy-start.3
  9.4 2.3 copy-start.6
  9.5 89.8 %all-gather.9.cloned.1.call-start = ((), (), s32[]{:S(2)}) async-start(), calls=%async_computation.8 | async-start | bytes 4128768 | tf_op jit(solution)/shard_map/all_gather | solution.py:56
  10.2 163.0 %all-gather.5.cloned.1.call-start = ((), (), s32[]{:S(2)}) async-start(), calls=%async_computation.6 | async-start | bytes 8257536 | tf_op jit(solution)/shard_map/all_gather | solution.py:51
  10.9 235.9 %all-gather.7.cloned.1.call-start = ((), (), s32[]{:S(2)}) async-start(), calls=%async_computation.7 | async-start | bytes 8257536 | tf_op jit(solution)/shard_map/all_gather | solution.py:52
  14.0 32.1 %all-to-all-start.3 = ((bf16[4,80,3584]{2,1,0:T(8,128)(2,1)}), bf16[4,80,3584]{2,1,0:T(8,128)(2,1)S(1)}, u32[]{:S(2)}, u32[]{:S(2)}) async-start(bf16[4,80,3584]{2,1,0:T(8,128)(2,1)} %bitcast.17), calls=%async_computation.3 | async-start | bytes 4587520 | tf_op jit(solution)/shard_map/all_to_all | solution.py:42
  46.2 1.5 copy-start.5
  47.6 56.9 %all-to-all-start = ((bf16[4,80,3584]{2,1,0:T(8,128)(2,1)}), bf16[4,80,3584]{2,1,0:T(8,128)(2,1)S(1)}, u32[]{:S(2)}, u32[]{:S(2)}) async-start(bf16[4,80,3584]{2,1,0:T(8,128)(2,1)} %bitcast.5), calls=%async_computation | async-start | bytes 4587520 | tf_op jit(solution)/shard_map/all_to_all | solution.py:42
  246.8 7.2 %copy-start.7 = (bf16[1,1024,1792]{2,1,0:T(8,128)(2,1)S(1)}, bf16[1,1024,1792]{2,1,0:T(8,128)(2,1)}, u32[]{:S(2)}) copy-start(bf16[1,1024,1792]{2,1,0:T(8,128)(2,1)} %all-gather.9.cloned.1.call-done) | copy-start | bytes 11010052
  254.1 2.5 copy-start.9
  256.5 18.9 %all-to-all-start.1 = ((bf16[4,80,1792]{2,1,0:T(8,128)(2,1)}), bf16[4,80,1792]{2,1,0:T(8,128)(2,1)S(1)}, u32[]{:S(2)}, u32[]{:S(2)}) async-start(bf16[4,80,1792]{2,1,0:T(8,128)(2,1)} %bitcast.10), calls=%async_computation.1 | async-start | bytes 2293760 | tf_op jit(solution)/shard_map/all_to_all | solution.py:42
  260.2 6.6 %copy-start.10 = (f32[320,1024]{1,0:T(8,128)S(1)}, f32[320,1024]{1,0:T(8,128)}, u32[]{:S(2)}) copy-start(f32[320,1024]{1,0:T(8,128)} %fusion.28) | copy-start | bytes 3932164
  260.2 6.6 %copy-start.11 = (f32[320,1024]{1,0:T(8,128)S(1)}, f32[320,1024]{1,0:T(8,128)}, u32[]{:S(2)}) copy-start(f32[320,1024]{1,0:T(8,128)} %fusion.6) | copy-start | bytes 3932164
  260.2 6.6 %copy-start.12 = (f32[320,1024]{1,0:T(8,128)S(1)}, f32[320,1024]{1,0:T(8,128)}, u32[]{:S(2)}) copy-start(f32[320,1024]{1,0:T(8,128)} %get-tuple-element.10) | copy-start | bytes 3932164
  275.4 1.0 copy-start.1
  276.4 30.2 %all-to-all-start.4 = ((bf16[4,80,3584]{2,1,0:T(8,128)(2,1)}), bf16[4,80,3584]{2,1,0:T(8,128)(2,1)S(1)}, u32[]{:S(2)}, u32[]{:S(2)}) async-start(bf16[4,80,3584]{2,1,0:T(8,128)(2,1)} %bitcast.82), calls=%async_computation.4 | async-start | bytes 4587520 | tf_op jit(solution)/shard_map/all_to_all | solution.py:42
  306.6 18.5 %all-to-all-start.2 = ((bf16[4,80,1792]{2,1,0:T(8,128)(2,1)}), bf16[4,80,1792]{2,1,0:T(8,128)(2,1)}, u32[]{:S(2)}, u32[]{:S(2)}) async-start(bf16[4,80,1792]{2,1,0:T(8,128)(2,1)} %bitcast.83), calls=%async_computation.2 | async-start | bytes 2293760 | tf_op jit(solution)/shard_map/all_to_all | solution.py:42
  312.8 15.9 %copy-start.4 = (bf16[1,128,3584]{2,1,0:T(8,128)(2,1)S(1)}, bf16[1,128,3584]{2,1,0:T(8,128)(2,1)}, u32[]{:S(2)}) copy-start(bf16[1,128,3584]{2,1,0:T(8,128)(2,1)} %param.8) | copy-start | bytes 2752516
  325.1 27.3 %all-to-all-start.5 = ((bf16[8,448,128]{2,1,0:T(8,128)(2,1)}), bf16[8,448,128]{2,1,0:T(8,128)(2,1)S(1)}, u32[]{:S(2)}, u32[]{:S(2)}) async-start(bf16[8,448,128]{2,1,0:T(8,128)(2,1)} %bitcast.75), calls=%async_computation.5 | async-start | bytes 1835008 | tf_op jit(solution)/shard_map/all_to_all | solution.py:82
  328.6 1.3 copy-start.2
Sparse Core Ops, SparseCore 0:
  10.2 45.2 all-gather.10
  57.8 41.4 all-gather.8
  100.9 72.2 all-gather.4
  174.7 72.0 all-gather.6
where the time goes:
time: 362 us; the launch traced here: 361 us
  waiting for transfers between devices  260 us (72%)
  matrix products  53.6 us (15%)
  starting transfers between devices  24.1 us (7%)
  between operations  14 us (4%)
  local copies, waits for them, and re-layouts  7.67 us (2%)
    all_gather x1, waiting for transfers between devices, local(): gate_matrix = lax.all_gather(w_gate, 'dp', axis=1, tiled=True)[0]  68.7 us
    all_gather x1, waiting for transfers between devices, local(): up_matrix = lax.all_gather(w_up, 'dp', axis=1, tiled=True)[0]  66.9 us
    all_to_all x5, waiting for transfers between devices, over_experts(): lax.all_to_all(rows.reshape(expert_count, capacity, cols), 'expert', spli...  60.3 us
    dot_general x13, matrix products, mm(): return lax.dot_general(a, b, dims, preferred_element_type=F32)  53.6 us
    all_gather x2, waiting for transfers between devices, local(): lax.all_gather(w_down[:, :, s], 'dp', axis=1, tiled=True)[0]  43.2 us
    all_to_all x5, starting transfers between devices, over_experts(): lax.all_to_all(rows.reshape(expert_count, capacity, cols), 'expert', spli...  20.4 us
    all_to_all x1, waiting for transfers between devices, local(): heads = lax.all_to_all(parts, 'dp', split_axis=0, concat_axis=0, tiled=True)  18.6 us
  transfers between devices with their start and end apart: 10, of which 9 were waited for; matrix products, arithmetic and copies ran while one was open for 13% of the time, Pallas kernels for 0%

commit v1 on v0

--- a/solution.py
+++ b/solution.py
@@ -6,6 +6,28 @@
 F32 = jnp.float32
 BF16 = jnp.bfloat16
 DOWN_PARTS = 2
+
+
+def laid_out(pieces, dim):
+    shape = list(pieces.shape[1:])
+    shape[dim] *= pieces.shape[0]
+    return jnp.moveaxis(pieces, 0, dim).reshape(shape)
+
+
+def gather_around(x, axis, dim):
+    size = lax.axis_size(axis)
+    pairs = [(i, (i + 1) % size) for i in range(size)]
+    back = [(b, a) for a, b in pairs]
+    lower, upper = ([], [])
+    for turn in range(size - 1):
+        if turn % 2 == 0:
+            lower.append(lax.ppermute(lower[-1] if lower else x, axis, pairs))
+        else:
+            upper.append(lax.ppermute(upper[-1] if upper else x, axis, back))
+    blocks = jnp.stack([*lower[::-1], x, *upper])
+    shift = lax.axis_index(axis) - len(lower)
+    blocks = blocks[(jnp.arange(size) - shift) % size]
+    return laid_out(blocks, dim)
 
 
 def placement(route_line, expert_count, capacity):
@@ -53,7 +75,7 @@
     w_down, _ = lax.optimization_barrier((w_down, gate_matrix[:16, :128]))
     step = width // DOWN_PARTS
     spans = [slice(i * step, (i + 1) * step) for i in range(DOWN_PARTS)]
-    downs = [lax.all_gather(w_down[:, :, s], "dp", axis=1, tiled=True)[0] for s in spans]
+    downs = [gather_around(w_down[:, :, s], "dp", 1)[0] for s in spans]
     routed = over_experts(mm(place, tokens[0]).astype(BF16))
     routed_grad = over_experts(mm(place, scaled_grad).astype(BF16))
     gate_pre = mm(routed, gate_matrix)

time: 362 us -> 324 us (0.90)
  waiting for transfers between devices: 260 us -> 131 us
  starting transfers between devices: 24.1 us -> 92.6 us
  local copies, waits for them, and re-layouts: 7.67 us -> 31.8 us
    ppermute x0 -> x14, starting transfers between devices: none -> 69.7 us  [the longest x6 50.3 us: gather_around(): upper.append(lax.ppermute(upper[-1] if upper else x, axis, back))]
    all_gather x1, waiting for transfers between devices: 68.7 us -> 0.01 us  [local(): gate_matrix = lax.all_gather(w_gate, 'dp', axis=1, tiled=True)[0]]
    all_gather x1, waiting for transfers between devices: 66.9 us -> 13.8 us  [local(): up_matrix = lax.all_gather(w_up, 'dp', axis=1, tiled=True)[0]]
    ppermute x0 -> x14, waiting for transfers between devices: none -> 49.4 us  [the longest x8 36.2 us: gather_around(): lower.append(lax.ppermute(lower[-1] if lower else x, axis, pairs))]
    all_gather x2 -> x0, waiting for transfers between devices: 43.2 us -> none  [local(): lax.all_gather(w_down[:, :, s], 'dp', axis=1, tiled=True)[0]]
    unnamed x26 -> x43, local copies, waits for them, and re-layouts: 3.56 us -> 18 us
    all_to_all x5, waiting for transfers between devices: 60.3 us -> 46.7 us  [over_experts(): lax.all_to_all(rows.reshape(expert_count, capacity, cols), 'expert', spli...]
    gather x0 -> x2, local copies, waits for them, and re-layouts: none -> 9.42 us  [gather_around(): blocks = blocks[(jnp.arange(size) - shift) % size]]
  transfers between devices with their start and end apart: 10 -> 22, of which waited for: 9 -> 12; matrix products, arithmetic and copies ran while one was open for 13% -> 22% of each run, Pallas kernels for 0% -> 0%
where the time goes in v1:
time: 324 us; the launch traced here: 323 us
  waiting for transfers between devices  131 us (40%)
  starting transfers between devices  92.6 us (29%)
  matrix products  50 us (15%)
  local copies, waits for them, and re-layouts  31.8 us (10%)
  between operations  14.3 us (4%)
    ppermute x6, starting transfers between devices, gather_around(): upper.append(lax.ppermute(upper[-1] if upper else x, axis, back))  50.3 us
    dot_general x13, matrix products, mm(): return lax.dot_general(a, b, dims, preferred_element_type=F32)  50 us
    all_to_all x5, waiting for transfers between devices, over_experts(): lax.all_to_all(rows.reshape(expert_count, capacity, cols), 'expert', spli...  46.7 us
    ppermute x8, waiting for transfers between devices, gather_around(): lower.append(lax.ppermute(lower[-1] if lower else x, axis, pairs))  36.2 us
    all_to_all x1, waiting for transfers between devices, local(): heads = lax.all_to_all(parts, 'dp', split_axis=0, concat_axis=0, tiled=True)  19.8 us
    ppermute x8, starting transfers between devices, gather_around(): lower.append(lax.ppermute(lower[-1] if lower else x, axis, pairs))  19.3 us
    all_to_all x5, starting transfers between devices, over_experts(): lax.all_to_all(rows.reshape(expert_count, capacity, cols), 'expert', spli...  19.1 us
    unnamed x43, local copies, waits for them, and re-layouts  18 us
  transfers between devices with their start and end apart: 22, of which 12 were waited for; matrix products, arithmetic and copies ran while one was open for 22% of the time, Pallas kernels for 0%

profile of v1, /device:TPU:0, one launch (start us, length us, event | category | flops | bytes accessed | tf_op | source)
XLA Modules:
  0.0 322.8 jit_solution(11730055464584579009)
XLA Ops:
  10.0 2.7 collective-permute-start.7
  12.7 7.7 %collective-permute-done = bf16[1,128,1792]{2,1,0:T(8,128)(2,1)S(1)} collective-permute-done((bf16[1,128,1792]{2,1,0:T(8,128)(2,1)}, bf16[1,128,1792]{2,1,0:T(8,128)(2,1)S(1)}, u32[]{:S(2)}, u32[]{:S(2)}) %collective-permute-start) | collective-permute-done | bytes 458784 | tf_op jit(solution)/shard_map/ppermute | solution.py:24
  20.4 3.5 %collective-permute-start.4 = (bf16[1,128,1792]{2,1,0:T(8,128)(2,1)}, bf16[1,128,1792]{2,1,0:T(8,128)(2,1)}, u32[]{:S(2)}, u32[]{:S(2)}) collective-permute-start(bf16[1,128,1792]{2,1,0:T(8,128)(2,1)} %get-tuple-element.9), channel_id=1, source_target_pairs={{4,0},{8,4},{12,8},{16,12},{20,16},{24,20},{28,24},{0,28},{5,1},{9... | collective-permute-start | bytes 1376264 | tf_op jit(solution)/shard_map/ppermute | solution.py:26
  24.2 1.5 collective-permute-done.7
  25.7 2.1 collective-permute-start.8
  27.7 17.6 %collective-permute-done.1 = bf16[1,128,1792]{2,1,0:T(8,128)(2,1)} collective-permute-done((bf16[1,128,1792]{2,1,0:T(8,128)(2,1)S(1)}, bf16[1,128,1792]{2,1,0:T(8,128)(2,1)}, u32[]{:S(2)}, u32[]{:S(2)}) %collective-permute-start.1) | collective-permute-done | bytes 458784 | tf_op jit(solution)/shard_map/ppermute | solution.py:24
  45.3 2.1 collective-permute-start.2
  47.4 2.2 convolution_convert_fusion
  49.6 4.5 %all-to-all-start.3 = ((bf16[4,80,3584]{2,1,0:T(8,128)(2,1)}), bf16[4,80,3584]{2,1,0:T(8,128)(2,1)}, u32[]{:S(2)}, u32[]{:S(2)}) async-start(bf16[4,80,3584]{2,1,0:T(8,128)(2,1)} %bitcast.36), calls=%async_computation.3 | async-start | bytes 4587520 | tf_op jit(solution)/shard_map/all_to_all | solution.py:64
  54.1 2.6 collective-permute-start.5
  56.7 7.8 %collective-permute-done.11 = bf16[1,128,1792]{2,1,0:T(8,128)(2,1)} collective-permute-done((bf16[1,128,1792]{2,1,0:T(8,128)(2,1)S(1)}, bf16[1,128,1792]{2,1,0:T(8,128)(2,1)}, u32[]{:S(2)}, u32[]{:S(2)}) %collective-permute-start.11) | collective-permute-done | bytes 458784 | tf_op jit(solution)/shard_map/ppermute | solution.py:26
  64.5 15.8 %collective-permute-start.12 = (bf16[1,128,1792]{2,1,0:T(8,128)(2,1)}, bf16[1,128,1792]{2,1,0:T(8,128)(2,1)S(1)}, u32[]{:S(2)}, u32[]{:S(2)}) collective-permute-start(bf16[1,128,1792]{2,1,0:T(8,128)(2,1)} %collective-permute-done.11), channel_id=1, source_target_pairs={{4,0},{8,4},{12,8},{16,12},{20,16},{24,20},{28,24},{0,28},{5,1},{9... | collective-permute-start | bytes 1376264 | tf_op jit(solution)/shard_map/ppermute | solution.py:26
  80.3 10.3 %collective-permute-start.9 = (bf16[1,128,1792]{2,1,0:T(8,128)(2,1)}, bf16[1,128,1792]{2,1,0:T(8,128)(2,1)S(1)}, u32[]{:S(2)}, u32[]{:S(2)}) collective-permute-start(bf16[1,128,1792]{2,1,0:T(8,128)(2,1)} %collective-permute-done.8), channel_id=1, source_target_pairs={{0,4},{4,8},{8,12},{12,16},{16,20},{20,24},{24,28},{28,0},{1,5},{5... | collective-permute-start | bytes 1376264 | tf_op jit(solution)/shard_map/ppermute | solution.py:24
  90.7 1.7 collective-permute-start.3
  92.4 2.2 convolution_convert_fusion.1
  94.7 1.8 collective-permute-start.6
  96.5 5.4 %collective-permute-done.12 = bf16[1,128,1792]{2,1,0:T(8,128)(2,1)S(1)} collective-permute-done((bf16[1,128,1792]{2,1,0:T(8,128)(2,1)}, bf16[1,128,1792]{2,1,0:T(8,128)(2,1)S(1)}, u32[]{:S(2)}, u32[]{:S(2)}) %collective-permute-start.12) | collective-permute-done | bytes 458784 | tf_op jit(solution)/shard_map/ppermute | solution.py:26
  101.8 26.6 %collective-permute-start.13 = (bf16[1,128,1792]{2,1,0:T(8,128)(2,1)S(1)}, bf16[1,128,1792]{2,1,0:T(8,128)(2,1)S(1)}, u32[]{:S(2)}, u32[]{:S(2)}) collective-permute-start(bf16[1,128,1792]{2,1,0:T(8,128)(2,1)S(1)} %collective-permute-done.12), channel_id=1, source_target_pairs={{4,0},{8,4},{12,8},{16,12},{20,16},{24,20},{28,24},{0,28},{5,1},{9... | collective-permute-start | bytes 1376264 | tf_op jit(solution)/shard_map/ppermute | solution.py:26
  129.3 1.8 bitcast_dynamic-update-slice_fusion.14
  131.1 1.8 bitcast_dynamic-update-slice_fusion.13
  133.7 9.4 %collective-permute-done.10 = bf16[1,128,1792]{2,1,0:T(8,128)(2,1)S(1)} collective-permute-done((bf16[1,128,1792]{2,1,0:T(8,128)(2,1)S(1)}, bf16[1,128,1792]{2,1,0:T(8,128)(2,1)S(1)}, u32[]{:S(2)}, u32[]{:S(2)}) %collective-permute-start.10) | collective-permute-done | bytes 458784 | tf_op jit(solution)/shard_map/ppermute | solution.py:24
  144.7 1.9 bitcast_dynamic-update-slice_fusion.5
  146.6 1.8 bitcast_dynamic-update-slice_fusion.4
  149.5 1.8 bitcast_dynamic-update-slice_fusion.10
  152.9 4.7 %gather_fusion = bf16[8,128,1792]{2,1,0:T(8,128)(2,1)} fusion(bf16[8,128,1792]{2,1,0:T(8,128)(2,1)} %bitcast.17, s32[1024]{0:T(1024)S(1)} %pad_clamp_fusion), kind=kCustom, calls=%fused_computation | custom fusion | bytes 7340064 | tf_op jit(solution)/shard_map/gather | solution.py:29
  157.7 1.9 bitcast_dynamic-update-slice_fusion.2
  159.5 3.8 %all-to-all-start = ((bf16[4,80,3584]{2,1,0:T(8,128)(2,1)}), bf16[4,80,3584]{2,1,0:T(8,128)(2,1)S(1)}, u32[]{:S(2)}, u32[]{:S(2)}) async-start(bf16[4,80,3584]{2,1,0:T(8,128)(2,1)} %bitcast.5), calls=%async_computation | async-start | bytes 4587520 | tf_op jit(solution)/shard_map/all_to_all | solution.py:64
  165.0 4.7 %gather_fusion.1 = bf16[8,128,1792]{2,1,0:T(8,128)(2,1)} fusion(bf16[8,128,1792]{2,1,0:T(8,128)(2,1)} %bitcast.30, s32[1024]{0:T(1024)S(1)} %pad_clamp_fusion), kind=kCustom, calls=%fused_computation.1 | custom fusion | bytes 7340064 | tf_op jit(solution)/shard_map/gather | solution.py:29
  169.7 4.0 %fusion.16 = f32[320,1024]{1,0:T(8,128)S(1)} fusion(bf16[1024,1792]{1,0:T(8,128)(2,1)} %bitcast.106, bf16[320,3584]{1,0:T(8,128)(2,1)} %bitcast.37), kind=kOutput, calls=%fused_computation.25 | convolution fusion | flops 1174405120 | bytes 6127616 | tf_op jit(solution)/shard_map/dot_general | solution.py:44
  173.7 3.8 %convolution_add_fusion = f32[320,1024]{1,0:T(8,128)} fusion(f32[320,1024]{1,0:T(8,128)S(1)} %fusion.16, bf16[1024,1792]{1,0:T(8,128)(2,1)S(1)} %bitcast.105, bf16[320,3584]{1,0:T(8,128)(2,1)} %bitcast.37), kind=kOutput, calls=%fused_computation.18 | convolution fusion | flops 1174732800 | bytes 7438336 | tf_op jit(solution)/shard_map/dot_general | solution.py:44
  177.5 11.2 %all-to-all-done = bf16[4,80,3584]{2,1,0:T(8,128)(2,1)S(1)} async-done(((bf16[4,80,3584]{2,1,0:T(8,128)(2,1)}), bf16[4,80,3584]{2,1,0:T(8,128)(2,1)S(1)}, u32[]{:S(2)}, u32[]{:S(2)}) %all-to-all-start) | async-done | bytes 2293792 | tf_op jit(solution)/shard_map/all_to_all | solution.py:64
  188.7 6.8 %fusion.6 = f32[320,1024]{1,0:T(8,128)} fusion(bf16[320,3584]{1,0:T(8,128)(2,1)S(1)} %bitcast.108, bf16[1,3584,1024]{2,1,0:T(8,128)(2,1)} %all-gather.3.cloned.1.call-done), kind=kOutput, calls=%fused_computation.8 | convolution fusion | flops 2348810240 | bytes 10944512 | tf_op jit(solution)/shard_map/dot_general | solution.py:44
  195.5 13.8 %all-gather.5.cloned.1.call-done = bf16[1,3584,1024]{2,1,0:T(8,128)(2,1)} async-done(((bf16[1,448,1024]{2,1,0:T(8,128)(2,1)}), bf16[1,3584,1024]{2,1,0:T(8,128)(2,1)}) %all-gather.5.cloned.1.call-update) | async-done | bytes 7340048 | tf_op jit(solution)/shard_map/all_gather | solution.py:74
  209.3 7.3 %multiply_convert_fusion.3 = (bf16[320,1024]{1,0:T(8,128)(2,1)S(1)}, f32[320,1024]{1,0:T(8,128)}) fusion(f32[320,1024]{1,0:T(8,128)} %fusion.6, bf16[320,3584]{1,0:T(8,128)(2,1)S(1)} %bitcast.109, bf16[1,3584,1024]{2,1,0:T(8,128)(2,1)} %all-gather.5.cloned.1.call-done), kind=kOutput, calls=%fused_computation.21 | convolution fusion | flops 2350776320 | bytes 12910592 | tf_op jit(solution)/shard_map/dot_general | solution.py:44
  216.6 2.4 convolution_convert_fusion.4
  219.0 3.7 %all-to-all-start.1 = ((bf16[4,80,1792]{2,1,0:T(8,128)(2,1)}), bf16[4,80,1792]{2,1,0:T(8,128)(2,1)S(1)}, u32[]{:S(2)}, u32[]{:S(2)}) async-start(bf16[4,80,1792]{2,1,0:T(8,128)(2,1)} %bitcast.20), calls=%async_computation.1 | async-start | bytes 2293760 | tf_op jit(solution)/shard_map/all_to_all | solution.py:64
  222.7 6.6 %fusion = f32[320,3584]{1,0:T(8,128)S(1)} fusion(bf16[1,3584,1024]{2,1,0:T(8,128)(2,1)} %all-gather.5.cloned.1.call-done, f32[320,1024]{1,0:T(8,128)} %convolution_add_fusion, f32[320,1024]{1,0:T(8,128)} %fusion.6), kind=kOutput, calls=%fused_computation.2 | convolution fusion | flops 2350776320 | bytes 14548992 | tf_op jit(solution)/shard_map/dot_general | solution.py:44
  229.3 7.4 %fusion.11 = bf16[320,3584]{1,0:T(8,128)(2,1)} fusion(f32[320,3584]{1,0:T(8,128)S(1)} %fusion, bf16[1,3584,1024]{2,1,0:T(8,128)(2,1)} %all-gather.3.cloned.1.call-done, f32[320,1024]{1,0:T(8,128)S(1)} %copy-done.13, f32[320,1024]{1,0:T(8,128)S(1)} %copy-done.12, f32[320,1024]{1,0:T(8,128)S(1)} %copy-done.14), kind=kOutput, calls=%fused_computation.11 | convolution fusion | flops 2354380800 | bytes 18153472 | tf_op jit(solution)/shard_map/dot_general | solution.py:44
  238.8 3.6 %all-to-all-start.4 = ((bf16[4,80,3584]{2,1,0:T(8,128)(2,1)}), bf16[4,80,3584]{2,1,0:T(8,128)(2,1)S(1)}, u32[]{:S(2)}, u32[]{:S(2)}) async-start(bf16[4,80,3584]{2,1,0:T(8,128)(2,1)} %bitcast.110), calls=%async_computation.4 | async-start | bytes 4587520 | tf_op jit(solution)/shard_map/all_to_all | solution.py:64
  242.5 4.4 %convolution_convert_fusion.3 = bf16[320,1792]{1,0:T(8,128)(2,1)} fusion(bf16[320,1024]{1,0:T(8,128)(2,1)S(1)} %get-tuple-element.11, bf16[1024,1792]{1,0:T(8,128)(2,1)} %bitcast.104), kind=kOutput, calls=%fused_computation.15 | convolution fusion | flops 1174978560 | bytes 5472256 | tf_op jit(solution)/shard_map/dot_general | solution.py:44
  246.9 22.2 %all-to-all-done.4 = bf16[4,80,3584]{2,1,0:T(8,128)(2,1)S(1)} async-done(((bf16[4,80,3584]{2,1,0:T(8,128)(2,1)}), bf16[4,80,3584]{2,1,0:T(8,128)(2,1)S(1)}, u32[]{:S(2)}, u32[]{:S(2)}) %all-to-all-start.4) | async-done | bytes 2293792 | tf_op jit(solution)/shard_map/all_to_all | solution.py:64
  269.1 3.5 %all-to-all-start.2 = ((bf16[4,80,1792]{2,1,0:T(8,128)(2,1)}), bf16[4,80,1792]{2,1,0:T(8,128)(2,1)S(1)}, u32[]{:S(2)}, u32[]{:S(2)}) async-start(bf16[4,80,1792]{2,1,0:T(8,128)(2,1)} %bitcast.111), calls=%async_computation.2 | async-start | bytes 2293760 | tf_op jit(solution)/shard_map/all_to_all | solution.py:64
  272.6 1.9 convolution_convert_fusion.2
  274.5 12.2 %all-to-all-done.2 = bf16[4,80,1792]{2,1,0:T(8,128)(2,1)S(1)} async-done(((bf16[4,80,1792]{2,1,0:T(8,128)(2,1)}), bf16[4,80,1792]{2,1,0:T(8,128)(2,1)S(1)}, u32[]{:S(2)}, u32[]{:S(2)}) %all-to-all-start.2) | async-done | bytes 1146912 | tf_op jit(solution)/shard_map/all_to_all | solution.py:64
  286.7 3.7 %all-to-all-start.5 = ((bf16[8,448,128]{2,1,0:T(8,128)(2,1)}), bf16[8,448,128]{2,1,0:T(8,128)(2,1)S(1)}, u32[]{:S(2)}, u32[]{:S(2)}) async-start(bf16[8,448,128]{2,1,0:T(8,128)(2,1)} %bitcast.40), calls=%async_computation.5 | async-start | bytes 1835008 | tf_op jit(solution)/shard_map/all_to_all | solution.py:104
  290.4 1.4 bitcast_convert_fusion
  294.3 19.8 %all-to-all-done.5 = bf16[8,448,128]{2,1,0:T(8,128)(2,1)S(1)} async-done(((bf16[8,448,128]{2,1,0:T(8,128)(2,1)}), bf16[8,448,128]{2,1,0:T(8,128)(2,1)S(1)}, u32[]{:S(2)}, u32[]{:S(2)}) %all-to-all-start.5) | async-done | bytes 917536 | tf_op jit(solution)/shard_map/all_to_all | solution.py:104
  314.7 1.3 reshape.119
  (68 shorter events, 15.8 us)
Async XLA Ops:
  7.2 85.3 %copy-start = (bf16[1,128,3584]{2,1,0:T(8,128)(2,1)S(1)}, bf16[1,128,3584]{2,1,0:T(8,128)(2,1)}, u32[]{:S(2)}) copy-start(bf16[1,128,3584]{2,1,0:T(8,128)(2,1)} %param.7) | copy-start | bytes 2752516
  7.2 1.5 copy-start.4
  7.2 16.8 %copy-start.11 = (s32[1,128]{1,0:T(1,128)S(1)}, s32[1,128]{1,0:T(1,128)}, u32[]{:S(2)}) copy-start(s32[1,128]{1,0:T(1,128)} %param.9) | copy-start | bytes 1540
  7.2 40.2 %copy-start.10 = (f32[1,128]{1,0:T(1,128)S(1)}, f32[1,128]{1,0:T(1,128)}, u32[]{:S(2)}) copy-start(f32[1,128]{1,0:T(1,128)} %param.10) | copy-start | bytes 1540
  7.2 40.2 %copy-start.7 = (bf16[1,128,3584]{2,1,0:T(8,128)(2,1)S(1)}, bf16[1,128,3584]{2,1,0:T(8,128)(2,1)}, u32[]{:S(2)}) copy-start(bf16[1,128,3584]{2,1,0:T(8,128)(2,1)} %param.8) | copy-start | bytes 2752516
  7.2 181.4 %all-gather.3.cloned.1.call-start = ((), (), s32[]{:S(2)}) async-start(), calls=%async_computation.6 | async-start | bytes 8257536 | tf_op jit(solution)/shard_map/all_gather | solution.py:73
  8.0 201.3 %all-gather.5.cloned.1.call-start = ((), (), s32[]{:S(2)}) async-start(), calls=%async_computation.7 | async-start | bytes 8257536 | tf_op jit(solution)/shard_map/all_gather | solution.py:74
  9.5 10.9 %collective-permute-start = (bf16[1,128,1792]{2,1,0:T(8,128)(2,1)}, bf16[1,128,1792]{2,1,0:T(8,128)(2,1)S(1)}, u32[]{:S(2)}, u32[]{:S(2)}) collective-permute-start(bf16[1,128,1792]{2,1,0:T(8,128)(2,1)} %get-tuple-element.9), channel_id=1, source_target_pairs={{0,4},{4,8},{8,12},{12,16},{16,20},{20,24},{24,28},{28,0},{1,5},{5... | collective-permute-start | bytes 1376264 | tf_op jit(solution)/shard_map/ppermute | solution.py:24
  10.0 15.7 %collective-permute-start.7 = (bf16[1,128,1792]{2,1,0:T(8,128)(2,1)S(1)}, bf16[1,128,1792]{2,1,0:T(8,128)(2,1)}, u32[]{:S(2)}, u32[]{:S(2)}) collective-permute-start(bf16[1,128,1792]{2,1,0:T(8,128)(2,1)S(1)} %get-tuple-element.10), channel_id=1, source_target_pairs={{0,4},{4,8},{8,12},{12,16},{16,20},{20,24},{24,28},{28,0},{1,5},{5... | collective-permute-start | bytes 1376264 | tf_op jit(solution)/shard_map/ppermute | solution.py:24
  20.4 5.3 %copy-start.8 = (bf16[1,128,1792]{2,1,0:T(8,128)(2,1)}, bf16[1,128,1792]{2,1,0:T(8,128)(2,1)S(1)}, u32[]{:S(2)}) copy-start(bf16[1,128,1792]{2,1,0:T(8,128)(2,1)S(1)} %collective-permute-done) | copy-start | bytes 1376260
  20.4 24.9 %collective-permute-start.1 = (bf16[1,128,1792]{2,1,0:T(8,128)(2,1)S(1)}, bf16[1,128,1792]{2,1,0:T(8,128)(2,1)}, u32[]{:S(2)}, u32[]{:S(2)}) collective-permute-start(bf16[1,128,1792]{2,1,0:T(8,128)(2,1)S(1)} %collective-permute-done), channel_id=1, source_target_pairs={{0,4},{4,8},{8,12},{12,16},{16,20},{20,24},{24,28},{28,0},{1,5},{5... | collective-permute-start | bytes 1376264 | tf_op jit(solution)/shard_map/ppermute | solution.py:24
  20.4 33.7 %collective-permute-start.4 = (bf16[1,128,1792]{2,1,0:T(8,128)(2,1)}, bf16[1,128,1792]{2,1,0:T(8,128)(2,1)}, u32[]{:S(2)}, u32[]{:S(2)}) collective-permute-start(bf16[1,128,1792]{2,1,0:T(8,128)(2,1)} %get-tuple-element.9), channel_id=1, source_target_pairs={{4,0},{8,4},{12,8},{16,12},{20,16},{24,20},{28,24},{0,28},{5,1},{9... | collective-permute-start | bytes 1376264 | tf_op jit(solution)/shard_map/ppermute | solution.py:26
  24.0 40.6 %collective-permute-start.11 = (bf16[1,128,1792]{2,1,0:T(8,128)(2,1)S(1)}, bf16[1,128,1792]{2,1,0:T(8,128)(2,1)}, u32[]{:S(2)}, u32[]{:S(2)}) collective-permute-start(bf16[1,128,1792]{2,1,0:T(8,128)(2,1)S(1)} %get-tuple-element.10), channel_id=1, source_target_pairs={{4,0},{8,4},{12,8},{16,12},{20,16},{24,20},{28,24},{0,28},{5,1},{9... | collective-permute-start | bytes 1376264 | tf_op jit(solution)/shard_map/ppermute | solution.py:26
  25.7 54.6 %collective-permute-start.8 = (bf16[1,128,1792]{2,1,0:T(8,128)(2,1)}, bf16[1,128,1792]{2,1,0:T(8,128)(2,1)}, u32[]{:S(2)}, u32[]{:S(2)}) collective-permute-start(bf16[1,128,1792]{2,1,0:T(8,128)(2,1)} %collective-permute-done.7), channel_id=1, source_target_pairs={{0,4},{4,8},{8,12},{12,16},{16,20},{20,24},{24,28},{28,0},{1,5},{5... | collective-permute-start | bytes 1376264 | tf_op jit(solution)/shard_map/ppermute | solution.py:24
  45.3 45.3 %collective-permute-start.2 = (bf16[1,128,1792]{2,1,0:T(8,128)(2,1)}, bf16[1,128,1792]{2,1,0:T(8,128)(2,1)}, u32[]{:S(2)}, u32[]{:S(2)}) collective-permute-start(bf16[1,128,1792]{2,1,0:T(8,128)(2,1)} %collective-permute-done.1), channel_id=1, source_target_pairs={{0,4},{4,8},{8,12},{12,16},{16,20},{20,24},{24,28},{28,0},{1,5},{5... | collective-permute-start | bytes 1376264 | tf_op jit(solution)/shard_map/ppermute | solution.py:24
  49.6 109.9 %all-to-all-start.3 = ((bf16[4,80,3584]{2,1,0:T(8,128)(2,1)}), bf16[4,80,3584]{2,1,0:T(8,128)(2,1)}, u32[]{:S(2)}, u32[]{:S(2)}) async-start(bf16[4,80,3584]{2,1,0:T(8,128)(2,1)} %bitcast.36), calls=%async_computation.3 | async-start | bytes 4587520 | tf_op jit(solution)/shard_map/all_to_all | solution.py:64
  54.1 40.5 %collective-permute-start.5 = (bf16[1,128,1792]{2,1,0:T(8,128)(2,1)}, bf16[1,128,1792]{2,1,0:T(8,128)(2,1)S(1)}, u32[]{:S(2)}, u32[]{:S(2)}) collective-permute-start(bf16[1,128,1792]{2,1,0:T(8,128)(2,1)} %collective-permute-done.4), channel_id=1, source_target_pairs={{4,0},{8,4},{12,8},{16,12},{20,16},{24,20},{28,24},{0,28},{5,1},{9... | collective-permute-start | bytes 1376264 | tf_op jit(solution)/shard_map/ppermute | solution.py:26
  64.5 37.3 %collective-permute-start.12 = (bf16[1,128,1792]{2,1,0:T(8,128)(2,1)}, bf16[1,128,1792]{2,1,0:T(8,128)(2,1)S(1)}, u32[]{:S(2)}, u32[]{:S(2)}) collective-permute-start(bf16[1,128,1792]{2,1,0:T(8,128)(2,1)} %collective-permute-done.11), channel_id=1, source_target_pairs={{4,0},{8,4},{12,8},{16,12},{20,16},{24,20},{28,24},{0,28},{5,1},{9... | collective-permute-start | bytes 1376264 | tf_op jit(solution)/shard_map/ppermute | solution.py:26
  80.3 48.1 %collective-permute-start.9 = (bf16[1,128,1792]{2,1,0:T(8,128)(2,1)}, bf16[1,128,1792]{2,1,0:T(8,128)(2,1)S(1)}, u32[]{:S(2)}, u32[]{:S(2)}) collective-permute-start(bf16[1,128,1792]{2,1,0:T(8,128)(2,1)} %collective-permute-done.8), channel_id=1, source_target_pairs={{0,4},{4,8},{8,12},{12,16},{16,20},{20,24},{24,28},{28,0},{1,5},{5... | collective-permute-start | bytes 1376264 | tf_op jit(solution)/shard_map/ppermute | solution.py:24
  90.7 37.8 %collective-permute-start.3 = (bf16[1,128,1792]{2,1,0:T(8,128)(2,1)}, bf16[1,128,1792]{2,1,0:T(8,128)(2,1)S(1)}, u32[]{:S(2)}, u32[]{:S(2)}) collective-permute-start(bf16[1,128,1792]{2,1,0:T(8,128)(2,1)} %collective-permute-done.2), channel_id=1, source_target_pairs={{0,4},{4,8},{8,12},{12,16},{16,20},{20,24},{24,28},{28,0},{1,5},{5... | collective-permute-start | bytes 1376264 | tf_op jit(solution)/shard_map/ppermute | solution.py:24
  94.7 38.2 %copy-start.9 = (bf16[1,128,1792]{2,1,0:T(8,128)(2,1)S(1)}, bf16[1,128,1792]{2,1,0:T(8,128)(2,1)}, u32[]{:S(2)}) copy-start(bf16[1,128,1792]{2,1,0:T(8,128)(2,1)} %copy-done.8) | copy-start | bytes 1376260
  94.7 57.5 %collective-permute-start.6 = (bf16[1,128,1792]{2,1,0:T(8,128)(2,1)S(1)}, bf16[1,128,1792]{2,1,0:T(8,128)(2,1)S(1)}, u32[]{:S(2)}, u32[]{:S(2)}) collective-permute-start(bf16[1,128,1792]{2,1,0:T(8,128)(2,1)S(1)} %collective-permute-done.5), channel_id=1, source_target_pairs={{4,0},{8,4},{12,8},{16,12},{20,16},{24,20},{28,24},{0,28},{5,1},{9... | collective-permute-start | bytes 1376264 | tf_op jit(solution)/shard_map/ppermute | solution.py:26
  101.8 62.3 %collective-permute-start.13 = (bf16[1,128,1792]{2,1,0:T(8,128)(2,1)S(1)}, bf16[1,128,1792]{2,1,0:T(8,128)(2,1)S(1)}, u32[]{:S(2)}, u32[]{:S(2)}) collective-permute-start(bf16[1,128,1792]{2,1,0:T(8,128)(2,1)S(1)} %collective-permute-done.12), channel_id=1, source_target_pairs={{4,0},{8,4},{12,8},{16,12},{20,16},{24,20},{28,24},{0,28},{5,1},{9... | collective-permute-start | bytes 1376264 | tf_op jit(solution)/shard_map/ppermute | solution.py:26
  128.4 14.7 %collective-permute-start.10 = (bf16[1,128,1792]{2,1,0:T(8,128)(2,1)S(1)}, bf16[1,128,1792]{2,1,0:T(8,128)(2,1)S(1)}, u32[]{:S(2)}, u32[]{:S(2)}) collective-permute-start(bf16[1,128,1792]{2,1,0:T(8,128)(2,1)S(1)} %collective-permute-done.9), channel_id=1, source_target_pairs={{0,4},{4,8},{8,12},{12,16},{16,20},{20,24},{24,28},{28,0},{1,5},{5... | collective-permute-start | bytes 1376264 | tf_op jit(solution)/shard_map/ppermute | solution.py:24
  159.5 29.1 %all-to-all-start = ((bf16[4,80,3584]{2,1,0:T(8,128)(2,1)}), bf16[4,80,3584]{2,1,0:T(8,128)(2,1)S(1)}, u32[]{:S(2)}, u32[]{:S(2)}) async-start(bf16[4,80,3584]{2,1,0:T(8,128)(2,1)} %bitcast.5), calls=%async_computation | async-start | bytes 4587520 | tf_op jit(solution)/shard_map/all_to_all | solution.py:64
  169.7 4.0 %copy-start.5 = (bf16[8,128,1792]{2,1,0:T(8,128)(2,1)S(1)}, bf16[8,128,1792]{2,1,0:T(8,128)(2,1)}, u32[]{:S(2)}) copy-start(bf16[8,128,1792]{2,1,0:T(8,128)(2,1)} %gather_fusion.1) | copy-start | bytes 11010052
  209.3 7.3 %copy-start.6 = (bf16[8,128,1792]{2,1,0:T(8,128)(2,1)S(1)}, bf16[8,128,1792]{2,1,0:T(8,128)(2,1)}, u32[]{:S(2)}) copy-start(bf16[8,128,1792]{2,1,0:T(8,128)(2,1)} %gather_fusion) | copy-start | bytes 11010052
  219.0 18.9 %all-to-all-start.1 = ((bf16[4,80,1792]{2,1,0:T(8,128)(2,1)}), bf16[4,80,1792]{2,1,0:T(8,128)(2,1)S(1)}, u32[]{:S(2)}, u32[]{:S(2)}) async-start(bf16[4,80,1792]{2,1,0:T(8,128)(2,1)} %bitcast.20), calls=%async_computation.1 | async-start | bytes 2293760 | tf_op jit(solution)/shard_map/all_to_all | solution.py:64
  222.7 6.6 %copy-start.12 = (f32[320,1024]{1,0:T(8,128)S(1)}, f32[320,1024]{1,0:T(8,128)}, u32[]{:S(2)}) copy-start(f32[320,1024]{1,0:T(8,128)} %convolution_add_fusion) | copy-start | bytes 3932164
  222.7 6.6 %copy-start.13 = (f32[320,1024]{1,0:T(8,128)S(1)}, f32[320,1024]{1,0:T(8,128)}, u32[]{:S(2)}) copy-start(f32[320,1024]{1,0:T(8,128)} %fusion.6) | copy-start | bytes 3932164
  222.7 6.6 %copy-start.14 = (f32[320,1024]{1,0:T(8,128)S(1)}, f32[320,1024]{1,0:T(8,128)}, u32[]{:S(2)}) copy-start(f32[320,1024]{1,0:T(8,128)} %get-tuple-element.12) | copy-start | bytes 3932164
  237.8 1.0 copy-start.2
  238.8 30.2 %all-to-all-start.4 = ((bf16[4,80,3584]{2,1,0:T(8,128)(2,1)}), bf16[4,80,3584]{2,1,0:T(8,128)(2,1)S(1)}, u32[]{:S(2)}, u32[]{:S(2)}) async-start(bf16[4,80,3584]{2,1,0:T(8,128)(2,1)} %bitcast.110), calls=%async_computation.4 | async-start | bytes 4587520 | tf_op jit(solution)/shard_map/all_to_all | solution.py:64
  269.1 17.6 %all-to-all-start.2 = ((bf16[4,80,1792]{2,1,0:T(8,128)(2,1)}), bf16[4,80,1792]{2,1,0:T(8,128)(2,1)S(1)}, u32[]{:S(2)}, u32[]{:S(2)}) async-start(bf16[4,80,1792]{2,1,0:T(8,128)(2,1)} %bitcast.111), calls=%async_computation.2 | async-start | bytes 2293760 | tf_op jit(solution)/shard_map/all_to_all | solution.py:64
  286.7 5.1 %copy-start.3 = (bf16[4,80,1792]{2,1,0:T(8,128)(2,1)S(1)}, bf16[4,80,1792]{2,1,0:T(8,128)(2,1)}, u32[]{:S(2)}) copy-start(bf16[4,80,1792]{2,1,0:T(8,128)(2,1)} %copy-done.2) | copy-start | bytes 3440644
  286.7 27.4 %all-to-all-start.5 = ((bf16[8,448,128]{2,1,0:T(8,128)(2,1)}), bf16[8,448,128]{2,1,0:T(8,128)(2,1)S(1)}, u32[]{:S(2)}, u32[]{:S(2)}) async-start(bf16[8,448,128]{2,1,0:T(8,128)(2,1)} %bitcast.40), calls=%async_computation.5 | async-start | bytes 1835008 | tf_op jit(solution)/shard_map/all_to_all | solution.py:104
  293.3 22.7 %copy-start.1 = (bf16[1,128,3584]{2,1,0:T(8,128)(2,1)S(1)}, bf16[1,128,3584]{2,1,0:T(8,128)(2,1)}, u32[]{:S(2)}) copy-start(bf16[1,128,3584]{2,1,0:T(8,128)(2,1)} %param.7) | copy-start | bytes 2752516
Sparse Core Ops, SparseCore 0:
  9.7 123.0 all-gather.2
  134.5 74.7 all-gather.4
